TPU v7x, 32 devices: a whole 2x2x4 slice. The times are simulated.
32 devices in a mesh: snp: 2 (over y), samp: 16 (over z, x, core).
Axes of the slice: x: 2, y: 2, z: 4, core: 2. Of those that a mesh axis runs over, the one named last changes fastest.
Arguments:
- dosages: bfloat16 [12288, 1024], P('samp', 'snp'), may hold values from 0 to 2
- residual: float32 [12288], P('samp'), may hold values from -40 to 40
- pair_list: int32 [4, 2], replicated, may hold values from 0 to 3, as said below
- block_slot: int32 [4], replicated, may hold values from 0 to 3, as said below
- pair_counts: int32 [4], replicated, may hold values from 3072 to 12288, as said below
Outputs:
- epistasis_score: float32 [1024], P('snp')
Inputs may be any that keep to these rules, and one draw needn't show every extreme that they name: `pair_list`: block b is paired with block (b + 1) mod 4, each such pair listed once, in some order and orientation. Counting each pair at the snp group block_slot[first block] // 2, no group gets more than 4 pairs and one group gets exactly 4. A permutation: block b is stored in columns block_slot[b] * 256 onward, on snp group block_slot[b] // 2. Pair p uses the samples with index below pair_counts[p]; some pair uses all 12288.
All inputs are finite; a program needn't handle non-finite values.
Results may differ from a plain program's by a relative error of at most 0.0021.
Values may be sent and summed in bfloat16 or wider, within the bound.
A program may use at most 64 MiB of HBM per device.

v0:
```python
import math

import jax
import jax.numpy as jnp
from jax import lax
from jax.sharding import PartitionSpec as P

BLOCK = 256


def on_device(dosages, residual, pair_list, block_slot, pair_counts):
    local_rows = dosages.shape[0]
    groups = lax.axis_size("snp")
    shards = lax.axis_size("samp")
    total_rows = local_rows * shards
    blocks = block_slot.shape[0]
    num_pairs = pair_list.shape[0]
    highest = lax.Precision.HIGHEST
    gathered = lax.all_gather(dosages, "snp", axis=1, tiled=True)
    spread_sum = lax.psum(jnp.sum(residual * residual), "samp")
    spread_var = spread_sum / total_rows
    position = lax.axis_index("samp") * local_rows + jnp.arange(local_rows, dtype=jnp.int32)
    block_ids = jnp.arange(blocks, dtype=jnp.int32)
    slot_first = jnp.sum(
        (pair_list[:, 0:1] == block_ids[None, :]).astype(jnp.int32) * block_slot[None, :], axis=1
    )
    slot_second = jnp.sum(
        (pair_list[:, 1:2] == block_ids[None, :]).astype(jnp.int32) * block_slot[None, :], axis=1
    )
    group_id = lax.axis_index("snp")
    pair_ids = jnp.arange(num_pairs, dtype=jnp.int32)
    width_slots = (num_pairs + groups - 1) // groups
    wanted = group_id * width_slots + jnp.arange(width_slots, dtype=jnp.int32)
    picked = (pair_ids[:, None] == wanted[None, :]).astype(jnp.int32)
    live_slot = jnp.sum(picked, axis=0)
    first_at = jnp.sum(picked * slot_first[:, None], axis=0)
    second_at = jnp.sum(picked * slot_second[:, None], axis=0)
    count_at = jnp.sum(picked * pair_counts[:, None], axis=0)
    live_rows = (position[None, :] < count_at[:, None]).astype(jnp.float32) * live_slot[
        :, None
    ].astype(jnp.float32)
    weight_rows = residual[None, :] * live_rows

    def masked_block(operand):
        second_slot, live = operand
        right = lax.dynamic_slice_in_dim(gathered, second_slot * BLOCK, BLOCK, 1)
        right_sq = right * right
        return (right_sq.astype(jnp.float32) * live[:, None]).astype(jnp.bfloat16)

    masked = lax.map(masked_block, (second_at, live_rows))
    rows = BLOCK // shards

    def one_slot(slot, buffer):
        first_col = lax.dynamic_index_in_dim(first_at, slot, 0, keepdims=False) * BLOCK
        second_col = lax.dynamic_index_in_dim(second_at, slot, 0, keepdims=False) * BLOCK
        left = lax.dynamic_slice_in_dim(gathered, first_col, rows * lax.axis_size("samp"), 1)
        right = lax.dynamic_slice_in_dim(gathered, second_col, BLOCK, 1)
        row_weight = lax.dynamic_index_in_dim(weight_rows, slot, 0, keepdims=False)
        masked_slot = lax.dynamic_index_in_dim(masked, slot, 0, keepdims=False)
        weighted = (left.astype(jnp.float32) * row_weight[:, None]).astype(jnp.bfloat16)
        left_sq = left * left
        cross = jnp.einsum("si,sj->ij", weighted, right, preferred_element_type=jnp.float32)
        moment = jnp.einsum("si,sj->ij", left_sq, masked_slot, preferred_element_type=jnp.float32)
        stacked = jnp.stack([cross, moment], axis=1)[:, :, None, :]
        return lax.dynamic_update_slice_in_dim(buffer, stacked, slot, 2)

    start_buffer = jnp.zeros((rows * lax.axis_size("samp"), 2, width_slots, BLOCK), jnp.float32)
    shares = lax.psum_scatter(
        lax.fori_loop(0, width_slots, one_slot, start_buffer),
        "samp",
        scatter_dimension=0,
        tiled=True,
    )
    zvalue = shares[:, 0] / jnp.sqrt(spread_var * shares[:, 1] + 1e-06)
    row_sums = jnp.sum(zvalue, axis=2)
    col_sums = jnp.sum(zvalue, axis=0)
    live_float = live_slot.astype(jnp.float32)
    first_hot = (first_at[:, None] == block_ids[None, :]).astype(jnp.float32) * live_float[:, None]
    second_hot = (second_at[:, None] == block_ids[None, :]).astype(jnp.float32) * live_float[
        :, None
    ]
    by_column = jnp.dot(second_hot.T, col_sums, precision=highest)
    by_row = jnp.dot(first_hot.T, row_sums.T, precision=highest)
    row_start = lax.axis_index("samp") * rows
    placed = lax.dynamic_update_slice_in_dim(
        jnp.zeros((blocks, BLOCK), jnp.float32), by_row, row_start, 1
    )
    partial_scores = (by_column + placed).reshape(blocks * BLOCK)
    group_part = lax.psum_scatter(partial_scores, "snp", scatter_dimension=0, tiled=True)
    totals = lax.psum(group_part, "samp")
    return totals / math.sqrt(2 * BLOCK)


def solution(mesh):
    return jax.shard_map(
        on_device,
        mesh=mesh,
        in_specs=(P("samp", "snp"), P("samp"), P(), P(), P()),
        out_specs=P("snp"),
        check_vma=False,
    )
```

profile of v0, /device:TPU:0, one launch (start us, length us, event | category | flops | bytes accessed | tf_op | source)
XLA Modules:
  0.0 156.7 jit_solution(12194418596713878061)
XLA Ops:
  6.5 0.0 all-gather.2.cloned.1.call-start
  6.5 0.7 all-gather.2.cloned.1.call-update
  7.3 0.0 reduce-scatter.2.cloned.1.call-start
  7.3 0.8 slice_bitcast_fusion
  8.1 0.9 select_reduce_fusion.1
  9.0 0.9 select_reduce_fusion.4
  9.9 0.8 compare_select_fusion
  10.6 28.2 %all-gather.2.cloned.1.call-done = bf16[768,1024]{1,0:T(8,128)(2,1)} async-done(((bf16[768,512]{1,0:T(8,128)(2,1)}), bf16[768,1024]{1,0:T(8,128)(2,1)}) %all-gather.2.cloned.1.call-update) | async-done | bytes 1572880 | tf_op jit(solution)/shard_map/all_gather | solution.py:19
  38.8 4.9 %while.23 = (s32[]{:T(128)}, bf16[2,768,256]{2,1,0:T(8,128)(2,1)S(1)}, s32[2]{0:T(128)S(1)}, bf16[768,1024]{1,0:T(8,128)(2,1)}, f32[2,768]{1,0:T(2,128)S(1)}, /*...) while((s32[]{:T(128)}, bf16[2,768,256]{2,1,0:T(8,128)(2,1)S(1)}, s32[2]{0:T(128)S(1)}, ...), condition=%wide.region_7.0_spmd, body=%wide.region_6.0_spmd.sunk | while | flops 983046 | bytes 796835 | solution.py:50
  38.8 0.6 dynamic_slice.85
  40.1 1.2 fusion.35
  41.3 0.6 dynamic_slice.85
  42.5 1.2 fusion.35
  43.7 0.0 copy-start.1
  43.7 0.0 copy-start.2
  43.8 11.0 %while.24 = (s32[]{:T(128)}, f32[256,2,2,256]{3,0,1,2:T(8,128)S(1)}, s32[2]{0:T(128)S(1)}, bf16[768,1024]{1,0:T(8,128)(2,1)}, f32[2,768]{1,0:T(2,128)S(1)}, /*in...) while((s32[]{:T(128)}, ...), condition=%wide.region_9.10_spmd, body=%wide.region_8.9_spmd.sunk | while | flops 202637312 | bytes 3155701 | solution.py:69
  43.8 0.6 dynamic_slice.91
  45.0 0.6 dynamic_slice.92
  46.3 1.6 %convolution_bitcast_fusion.5 = f32[256,1,256]{2,0,1:T(8,128)S(1)} fusion(bf16[768,1024]{1,0:T(8,128)(2,1)} %get-tuple-element.320, s32[]{:T(128)S(6)} %select_n.38, f32[768]{0:T(1024)S(1)} %dynamic-slice_reduce_fusion.5, s32[]{:T(128)S(6)} %select_n.37), kind=kOutput, calls=%fused_computation.5.clone.1 | convolution fusion | flops 101253120 | bytes 1051656 | tf_op jit(solution)/shard_map/while/body/eval_jaxpr/si,sj->ij/dot_general | solution.py:62
  47.9 1.3 convolution_bitcast_fusion.4
  49.3 0.6 dynamic_slice.91
  50.5 0.6 dynamic_slice.92
  51.7 1.6 %convolution_bitcast_fusion.5 = f32[256,1,256]{2,0,1:T(8,128)S(1)} fusion(bf16[768,1024]{1,0:T(8,128)(2,1)} %get-tuple-element.320, s32[]{:T(128)S(6)} %select_n.38, f32[768]{0:T(1024)S(1)} %dynamic-slice_reduce_fusion.5, s32[]{:T(128)S(6)} %select_n.37), kind=kOutput, calls=%fused_computation.5.clone.1 | convolution fusion | flops 101253120 | bytes 1051656 | tf_op jit(solution)/shard_map/while/body/eval_jaxpr/si,sj->ij/dot_general | solution.py:62
  53.3 1.3 convolution_bitcast_fusion.4
  54.7 0.0 copy-start
  54.7 1.0 copy-done
  55.7 0.0 reduce-scatter.2.cloned.1.call-update
  55.7 0.0 copy-done.1
  55.7 0.6 multiply_reduce_fusion
  56.3 33.9 %psum.14 = f32[]{:T(128)} all-reduce(f32[]{:T(128)} %multiply_reduce_fusion), channel_id=1, replica_groups=mesh['snp'=2,'samp'=16] {'samp'}, use_global_device_ids=true, to_apply=%region_12.13 | all-reduce | flops 1 | bytes 8 | tf_op jit(solution)/shard_map/psum | solution.py:20
  90.9 0.0 copy-done.2
  90.9 0.6 dynamic-slice.1
  92.1 21.1 %reduce-scatter.2.cloned.1.call-done = f32[16,2,2,256]{3,0,1,2:T(8,128)} async-done(((f32[256,2,2,256]{3,0,1,2:T(8,128)}), f32[16,2,2,256]{3,0,1,2:T(8,128)}) %reduce-scatter.2.cloned.1.call-update) | async-done | bytes 65552 | tf_op jit(solution)/shard_map/reduce_scatter | solution.py:68
  113.3 0.9 fusion.15
  114.1 0.3 fusion.17
  114.4 0.3 convolution_add_fusion
  114.6 0.1 add.97
  114.8 4.9 %all-reduce = f32[1024]{0:T(1024)S(1)} all-reduce(f32[1024]{0:T(1024)S(1)} %bitcast.43), channel_id=3, replica_groups=mesh['snp'=2,'samp'=16] {'snp'}, use_global_device_ids=true, to_apply=%region_15.16.clone | all-reduce | flops 1024 | bytes 8192
  119.7 0.1 dynamic-slice.2
  119.8 29.5 %psum.15 = f32[512]{0:T(512)S(1)} all-reduce(f32[512]{0:T(512)S(1)} %dynamic-slice.2), channel_id=1, replica_groups=mesh['snp'=2,'samp'=16] {'samp'}, use_global_device_ids=true, to_apply=%region_16.17 | all-reduce | flops 512 | bytes 4096 | tf_op jit(solution)/shard_map/psum | solution.py:90
  149.3 0.6 broadcast_multiply_fusion.1
  (12 shorter events, 0.2 us)
Async XLA Ops:
  6.5 32.3 %all-gather.2.cloned.1.call-start = ((), (), s32[]{:S(2)}) async-start(), calls=%async_computation.1 | async-start | bytes 2359296 | tf_op jit(solution)/shard_map/all_gather | solution.py:19
  7.3 106.0 %reduce-scatter.2.cloned.1.call-start = ((), (), s32[]{:S(2)}) async-start(), calls=%async_computation.2 | async-start | bytes 1114112 | tf_op jit(solution)/shard_map/reduce_scatter | solution.py:68
  43.7 12.0 %copy-start.1 = (f32[768]{0:T(1024)S(1)}, f32[768]{0:T(1024)}, u32[]{:S(2)}) copy-start(f32[768]{0:T(1024)} %param.10) | copy-start | bytes 9220
  43.7 47.1 %copy-start.2 = (u32[32]{0:T(128)S(1)}, u32[32]{0:T(128)}, u32[]{:S(2)}) copy-start(u32[32]{0:T(128)} %constant.108) | copy-start | bytes 388
  54.7 1.0 copy-start
Sparse Core Ops, SparseCore 0:
  8.9 29.8 all-gather.1
  55.9 57.3 reduce-scatter.1
where the time goes:
time: 157 us
  blocking collectives  68.3 us (44%)
  waiting for transfers between devices  50.1 us (32%)
  between operations  14.8 us (9%)
  other arithmetic  7 us (4%)
  matrix products  6.34 us (4%)
  local copies, waits for them, and re-layouts  6.29 us (4%)
  loops' own time  3.83 us (2%)
    psum x1, blocking collectives, on_device(): spread_sum = lax.psum(jnp.sum(residual * residual), 'samp')  33.9 us
    psum x1, blocking collectives, on_device(): totals = lax.psum(group_part, 'samp')  29.5 us
    all_gather x1, waiting for transfers between devices, on_device(): gathered = lax.all_gather(dosages, 'snp', axis=1, tiled=True)  28.2 us
    reduce_scatter x1, waiting for transfers between devices, on_device(): lax.psum_scatter(lax.fori_loop(0, width_slots, one_slot, start_buffer), '...  21.1 us
    unnamed x1, blocking collectives  4.95 us
    dot_general x2, matrix products, one_slot(): jnp.einsum('si,sj->ij', weighted, right, preferred_element_type=jnp.float32)  3.19 us
  transfers between devices with their start and end apart: 2, of which 2 were waited for; matrix products, arithmetic and copies ran while one was open for 3% of the time, Pallas kernels for 0%

commit v1 on v0

--- a/solution.py
+++ b/solution.py
@@ -3,12 +3,14 @@
 import jax
 import jax.numpy as jnp
 from jax import lax
+from jax.experimental import pallas as pl
+from jax.experimental.pallas import tpu as pltpu
 from jax.sharding import PartitionSpec as P
 
 BLOCK = 256
 
 
-def on_device(dosages, residual, pair_list, block_slot, pair_counts):
+def any_groups(dosages, residual, pair_list, block_slot, pair_counts):
     local_rows = dosages.shape[0]
     groups = lax.axis_size("snp")
     shards = lax.axis_size("samp")
@@ -91,7 +93,234 @@
     return totals / math.sqrt(2 * BLOCK)
 
 
+CHUNKS = 2
+OFFSETS = [(dy, dz, dx, dc) for dy in range(2) for dz in range(4) for dx in range(2) for dc in range(2)]
+
+
+def flip(bit, change):
+    return 1 - bit if change else bit
+
+
+def two_groups_kernel(
+    list_ref, slot_ref, count_ref, dos_ref, res_ref, out_ref,
+    mine, other, weights, square_sum, cross, moment, moment_half, cross_in, moment_in, final, send_vec,
+    local_sem, mate_sem, mate_send, far_sem, far_send, res_sem, res_send,
+    sum_sem, sum_send, cross_sem, cross_send, moment_sem, moment_send, final_sem, final_send,
+):
+    y = lax.axis_index("snp")
+    k = lax.axis_index("samp")
+    z, x, c = k // 4, (k // 2) % 2, k % 2
+    rows = dos_ref.shape[0]
+    part = rows // CHUNKS
+    own = c + y - 2 * c * y
+    share = BLOCK // 8
+
+    def at(dy, dz, dx, dc):
+        return (flip(y, dy), ((z + dz) % 4 * 2 + flip(x, dx)) * 2 + flip(c, dc))
+
+    def column(block):
+        return pl.ds(pl.multiple_of(block * BLOCK, BLOCK), BLOCK)
+
+    def remote(src, dst, send, recv, to):
+        copy = pltpu.make_async_remote_copy(
+            src_ref=src, dst_ref=dst, send_sem=send, recv_sem=recv,
+            device_id=to, device_id_type=pl.DeviceIdType.MESH,
+        )
+        copy.start()
+        return copy
+
+    local = pltpu.make_async_copy(dos_ref.at[:, column(own)], mine.at[0], local_sem)
+    local.start()
+    barrier = pltpu.get_barrier_semaphore()
+    for offset in OFFSETS[1:]:
+        pl.semaphore_signal(
+            barrier, inc=1, device_id=at(*offset), device_id_type=pl.DeviceIdType.MESH
+        )
+    pl.semaphore_wait(barrier, len(OFFSETS) - 1)
+
+    far = []
+    for dc in range(2):
+        for part_id in range(CHUNKS):
+            span = pl.ds(part_id * part, part)
+            far.append(
+                remote(
+                    dos_ref.at[span, column(flip(c, dc))], other.at[dc, span],
+                    far_send.at[dc, part_id], far_sem.at[dc, part_id], at(1, 0, 0, dc),
+                )
+            )
+    near = [
+        remote(res_ref, weights, res_send, res_sem, at(0, 0, 0, 1)),
+        remote(dos_ref.at[:, column(1 - own)], mine.at[1], mate_send, mate_sem, at(0, 0, 0, 1)),
+    ]
+
+    own_slot, far_slot = 2 * y + own, 2 * (1 - y) + c
+    count = jnp.int32(0)
+    for pair in range(4):
+        first = slot_ref[list_ref[pair, 0]]
+        second = slot_ref[list_ref[pair, 1]]
+        here = ((first == own_slot) & (second == far_slot)) | (
+            (first == far_slot) & (second == own_slot)
+        )
+        count = count + jnp.where(here, count_ref[pair], 0)
+    hot_group = jnp.where(slot_ref[list_ref[0, 0]] >= 2, 1, 0)
+    hot_here = jnp.where(hot_group == y, 1, 0)
+
+    def products(dc, part_id):
+        span = pl.ds(part_id * part, part)
+        near_block = mine[dc, span, :]
+        far_block = other[dc, span, :]
+        pick = jnp.full((part, BLOCK), hot_here, jnp.int32) == 1
+        left = jnp.where(pick, near_block, far_block).T
+        right = jnp.where(pick, far_block, near_block)
+        base = (k - c + flip(c, dc)) * rows + part_id * part
+        live = (base + lax.broadcasted_iota(jnp.int32, (1, part), 1) < count).astype(jnp.float32)
+        source = res_ref if dc == 0 else weights
+        weight = source[:, span] * live
+        left_wide = left.astype(jnp.float32)
+        weighted = (left_wide * weight).astype(jnp.bfloat16)
+        left_sq = (left_wide * left_wide).astype(jnp.bfloat16)
+        masked = (left_sq.astype(jnp.float32) * live).astype(jnp.bfloat16)
+        right_wide = right.astype(jnp.float32)
+        right_sq = (right_wide * right_wide).astype(jnp.bfloat16)
+        return (
+            jnp.dot(weighted, right, preferred_element_type=jnp.float32),
+            jnp.dot(masked, right_sq, preferred_element_type=jnp.float32),
+        )
+
+    local.wait()
+    near[0].wait()
+    both = res_ref[...] * res_ref[...] + weights[...] * weights[...]
+    square_sum[0] = jnp.broadcast_to(jnp.sum(both, axis=1, keepdims=True), (8, 128))
+    ring = [offset for offset in OFFSETS[1:] if offset[0] == 0 and offset[3] == 0]
+    started = []
+    for place, offset in enumerate(ring):
+        started.append(
+            remote(
+                square_sum.at[0], square_sum.at[place + 1],
+                sum_send.at[place], sum_sem.at[place], at(*offset),
+            )
+        )
+    step = 0
+    for dc in range(2):
+        if dc == 1:
+            near[1].wait()
+        for part_id in range(CHUNKS):
+            far[step].wait()
+            cross_part, moment_part = products(dc, part_id)
+            if step == 0:
+                cross[...] = cross_part
+                moment[...] = moment_part
+            else:
+                cross[...] += cross_part
+                moment[...] += moment_part
+            step += 1
+    moment_half[...] = moment[...].astype(jnp.bfloat16)
+
+    def share_of(place):
+        return pl.ds(pl.multiple_of(place * share, share), share)
+
+    for place, offset in enumerate(ring):
+        to = at(*offset)
+        span = share_of(to[1] // 2)
+        started.append(
+            remote(
+                cross.at[span], cross_in.at[place],
+                cross_send.at[place], cross_sem.at[place], to,
+            )
+        )
+        started.append(
+            remote(
+                moment_half.at[span], moment_in.at[place],
+                moment_send.at[place], moment_sem.at[place], to,
+            )
+        )
+    for copy in started:
+        copy.wait()
+    span = share_of(k // 2)
+    cross_sum = cross[span, :]
+    moment_sum = moment[span, :]
+    squares = square_sum[0]
+    for place in range(len(ring)):
+        cross_sum += cross_in[place]
+        moment_sum += moment_in[place].astype(jnp.float32)
+        squares += square_sum[place + 1]
+    spread_var = squares[0:1, 0:1] / (rows * 16)
+    zvalue = cross_sum / jnp.sqrt(spread_var * moment_sum + 1e-06)
+    row_sums = jnp.sum(zvalue, axis=1, keepdims=True)
+    col_vec = jnp.sum(zvalue, axis=0, keepdims=True)
+    row_at = lax.broadcasted_iota(jnp.int32, (share, BLOCK), 0) + share * (k // 2)
+    spot = row_at == lax.broadcasted_iota(jnp.int32, (share, BLOCK), 1)
+    row_vec = jnp.sum(jnp.where(spot, row_sums, 0.0), axis=0, keepdims=True)
+    pick_row = jnp.full((1, BLOCK), hot_here, jnp.int32) == 1
+    send_vec[0] = jnp.where(pick_row, row_vec, col_vec)
+    send_vec[1] = jnp.where(pick_row, col_vec, row_vec)
+    started = []
+    for place, offset in enumerate(OFFSETS):
+        if place > 0:
+            started.append(
+                remote(
+                    send_vec.at[offset[0]], final.at[place],
+                    final_send.at[place], final_sem.at[place], at(*offset),
+                )
+            )
+    final[0] = send_vec[0]
+    for copy in started:
+        copy.wait()
+    total = {}
+    for place, offset in enumerate(OFFSETS):
+        key = (offset[0], offset[3])
+        total[key] = total[key] + final[place] if key in total else final[place]
+    swap_far = jnp.full((1, BLOCK), c, jnp.int32) == 1
+    swap_own = jnp.full((1, BLOCK), own, jnp.int32) == 1
+    scale = 1.0 / math.sqrt(2 * BLOCK)
+    for block in range(2):
+        same = jnp.where(swap_own, total[0, 1 - block], total[0, block])
+        cross_group = jnp.where(swap_far, total[1, 1 - block], total[1, block])
+        out_ref[block : block + 1, :] = (same + cross_group) * scale
+
+
+def two_groups(dosages, residual, pair_list, block_slot, pair_counts):
+    rows = dosages.shape[0]
+    dma = pltpu.SemaphoreType.DMA
+    peers = len(OFFSETS)
+    smem = pl.BlockSpec(memory_space=pltpu.SMEM)
+    vmem = pl.BlockSpec(memory_space=pltpu.VMEM)
+    score = pl.pallas_call(
+        two_groups_kernel,
+        out_shape=jax.ShapeDtypeStruct((2, BLOCK), jnp.float32),
+        in_specs=[smem, smem, smem, pl.BlockSpec(memory_space=pl.ANY), vmem],
+        out_specs=vmem,
+        scratch_shapes=[
+            pltpu.VMEM((2, rows, BLOCK), jnp.bfloat16),
+            pltpu.VMEM((2, rows, BLOCK), jnp.bfloat16),
+            pltpu.VMEM((1, rows), jnp.float32),
+            pltpu.VMEM((8, 8, 128), jnp.float32),
+            pltpu.VMEM((BLOCK, BLOCK), jnp.float32),
+            pltpu.VMEM((BLOCK, BLOCK), jnp.float32),
+            pltpu.VMEM((BLOCK, BLOCK), jnp.bfloat16),
+            pltpu.VMEM((7, BLOCK // 8, BLOCK), jnp.float32),
+            pltpu.VMEM((7, BLOCK // 8, BLOCK), jnp.bfloat16),
+            pltpu.VMEM((peers, 1, BLOCK), jnp.float32),
+            pltpu.VMEM((2, 1, BLOCK), jnp.float32),
+            dma, dma, dma, dma((2, CHUNKS)), dma((2, CHUNKS)), dma, dma,
+            dma((7,)), dma((7,)), dma((7,)), dma((7,)), dma((7,)), dma((7,)),
+            dma((peers,)), dma((peers,)),
+        ],
+        compiler_params=pltpu.CompilerParams(
+            collective_id=0, has_side_effects=True, vmem_limit_bytes=32 * 1024 * 1024
+        ),
+        name="pair_scores",
+    )(pair_list, block_slot, pair_counts, dosages, residual.reshape(1, rows))
+    return score.reshape(2 * BLOCK)
+
+
 def solution(mesh):
+    def on_device(dosages, residual, pair_list, block_slot, pair_counts):
+        groups, shards = lax.axis_size("snp"), lax.axis_size("samp")
+        fits = groups == 2 and shards == 16 and block_slot.shape[0] == 4
+        run = two_groups if fits else any_groups
+        return run(dosages, residual, pair_list, block_slot, pair_counts)
+
     return jax.shard_map(
         on_device,
         mesh=mesh,

time: 157 us -> 46.8 us (0.30)
  blocking collectives: 68.3 us -> 0 us
  waiting for transfers between devices: 50.1 us -> 0 us
  Pallas kernels: 0 us -> 43.4 us
  between operations: 14.8 us -> 0.02 us
  other arithmetic: 7 us -> 0 us
  matrix products: 6.34 us -> 0 us
  loops' own time: 3.83 us -> 0 us
  local copies, waits for them, and re-layouts: 6.29 us -> 3.2 us
    psum x2 -> x0, blocking collectives: 63.3 us -> none  [the longest x1 33.9 us: on_device(): spread_sum = lax.psum(jnp.sum(residual * residual), 'samp')]
    pallas_call x0 -> x1, Pallas kernels: none -> 43.4 us  [two_groups(): pl.pallas_call(two_groups_kernel, out_shape=jax.ShapeDtypeStruct((2, BLOC...]
    all_gather x1 -> x0, waiting for transfers between devices: 28.2 us -> none  [on_device(): gathered = lax.all_gather(dosages, 'snp', axis=1, tiled=True)]
    reduce_scatter x1 -> x0, waiting for transfers between devices: 21.1 us -> none  [on_device(): lax.psum_scatter(lax.fori_loop(0, width_slots, one_slot, start_buffer), '...]
    dot_general x6 -> x0, matrix products: 6.34 us -> none  [the longest x2 3.19 us: one_slot(): jnp.einsum('si,sj->ij', weighted, right, preferred_element_type=jnp.float32)]
    unnamed x1 -> x0, blocking collectives: 4.95 us -> none
    another operation x2 -> x0, loops' own time: 3.83 us -> none  [the longest x1 2.55 us: on_device(): lax.fori_loop(0, width_slots, one_slot, start_buffer)]
    dynamic_slice x10 -> x0, local copies, waits for them, and re-layouts: 3.77 us -> none  [the longest x4 1.27 us: on_device(): masked = lax.map(masked_block, (second_at, live_rows))]
  transfers between devices with their start and end apart: 2 -> 0, of which waited for: 2 -> 0; matrix products, arithmetic and copies ran while one was open for 3% -> 0% of each run, Pallas kernels for 0% -> 0%
where the time goes in v1:
time: 46.8 us; the launch traced here: 46.6 us
  Pallas kernels  43.4 us (93%)
  local copies, waits for them, and re-layouts  3.2 us (7%)
    pallas_call x1, Pallas kernels, two_groups(): pl.pallas_call(two_groups_kernel, out_shape=jax.ShapeDtypeStruct((2, BLOC...  43.4 us
    unnamed x8, local copies, waits for them, and re-layouts  2.48 us

profile of v1, /device:TPU:0, one launch (start us, length us, event | category | flops | bytes accessed | tf_op | source)
XLA Modules:
  0.0 46.6 jit_solution(5391397106807008215)
XLA Ops:
  0.0 0.8 %copy.6.list_ref = s32[4,2]{1,0:T(4,128)S(1)} copy(s32[4,2]{0,1:T(2,128)} %param.7) | data formatting | bytes 64 | tf_op args[2]
  0.8 0.0 copy-start.1
  0.8 0.0 copy-start.2
  0.8 0.7 %reshape.6.res_ref = f32[1,768]{1,0:T(1,128)S(1)} reshape(f32[768]{0:T(1024)} %param.6) | data formatting | bytes 6144 | tf_op jit(solution)/shard_map/reshape | solution.py:313
  1.5 0.0 copy-done.1
  1.5 0.0 copy-done.2
  1.5 0.0 copy-start
  1.5 1.1 %copy-done = bf16[768,512]{1,0:T(8,128)(2,1)S(1)} copy-done((bf16[768,512]{1,0:T(8,128)(2,1)S(1)}, bf16[768,512]{1,0:T(8,128)(2,1)}, u32[]{:S(2)}) %copy-start) | copy-done | bytes 786456
  2.6 43.4 %pair_scores.1 = f32[2,256]{1,0:T(2,128)S(1)} custom-call(s32[4,2]{1,0:T(4,128)S(1)} %copy.6.list_ref, s32[4]{0:T(128)S(1)} %copy-done.1, s32[4]{0:T(128)S(1)} %copy-done.2, bf16[768,512]{1,0:T(8,128)(2,1)S(1)} %copy-done, f32[1,768]{1,0:T(1,128)S(1)} %reshape.6.res_ref), custom_call_target="tpu_custom_call" | custom-call | tf_op jit(solution)/shard_map/pair_scores/pallas_call | solution.py:288
  46.0 0.6 %copy.7 = f32[1,2,2,128]{3,1,2,0:T(2,128)} copy(f32[1,2,2,128]{3,2,1,0:T(2,128)S(1)} %bitcast.2) | data formatting | bytes 4096
Async XLA Ops:
  0.8 0.7 %copy-start.1 = (s32[4]{0:T(128)S(1)}, s32[4]{0:T(128)}, u32[]{:S(2)}) copy-start(s32[4]{0:T(128)} %slot_ref.1) | copy-start | bytes 52
  0.8 0.7 %copy-start.2 = (s32[4]{0:T(128)S(1)}, s32[4]{0:T(128)}, u32[]{:S(2)}) copy-start(s32[4]{0:T(128)} %count_ref.1) | copy-start | bytes 52
  1.5 1.1 %copy-start = (bf16[768,512]{1,0:T(8,128)(2,1)S(1)}, bf16[768,512]{1,0:T(8,128)(2,1)}, u32[]{:S(2)}) copy-start(bf16[768,512]{1,0:T(8,128)(2,1)} %dos_ref.1) | copy-start | bytes 2359300

commit v2 on v0

--- a/solution.py
+++ b/solution.py
@@ -3,12 +3,14 @@
 import jax
 import jax.numpy as jnp
 from jax import lax
+from jax.experimental import pallas as pl
+from jax.experimental.pallas import tpu as pltpu
 from jax.sharding import PartitionSpec as P
 
 BLOCK = 256
 
 
-def on_device(dosages, residual, pair_list, block_slot, pair_counts):
+def any_groups(dosages, residual, pair_list, block_slot, pair_counts):
     local_rows = dosages.shape[0]
     groups = lax.axis_size("snp")
     shards = lax.axis_size("samp")
@@ -91,7 +93,238 @@
     return totals / math.sqrt(2 * BLOCK)
 
 
+HALVES = 2
+RING = [(0, dz, dx, 0) for dz in range(4) for dx in range(2)][1:]
+COLUMN = [(0, 0, 0, 1), (1, 0, 0, 0), (1, 0, 0, 1)]
+
+
+def flip(bit, change):
+    return 1 - bit if change else bit
+
+
+def two_groups_kernel(
+    list_hbm, slot_hbm, count_hbm, dos_ref, res_ref, out_ref,
+    list_ref, slot_ref, count_ref, mine, other, residuals, left_weighted, left_masked, right_weight,
+    square_sum, cross, moment, parts, parts_in, vecs, vecs_in, last, last_in,
+    local_sem, mate_sem, mate_send, far_sem, far_send, res_sem, res_send,
+    sum_sem, sum_send, part_sem, part_send, vec_sem, vec_send, last_sem, last_send,
+):
+    y = lax.axis_index("snp")
+    k = lax.axis_index("samp")
+    z, x, c = k // 4, (k // 2) % 2, k % 2
+    rows = dos_ref.shape[0]
+    own = c + y - 2 * c * y
+    share = BLOCK // 8
+    width = BLOCK // HALVES
+    mesh_id = pl.DeviceIdType.MESH
+
+    def at(dy, dz, dx, dc):
+        return (flip(y, dy), ((z + dz) % 4 * 2 + flip(x, dx)) * 2 + flip(c, dc))
+
+    def column(start, size):
+        return pl.ds(pl.multiple_of(start, 128), size)
+
+    def remote(src, dst, send, recv, to):
+        copy = pltpu.make_async_remote_copy(
+            src_ref=src, dst_ref=dst, send_sem=send, recv_sem=recv,
+            device_id=to, device_id_type=mesh_id,
+        )
+        copy.start()
+        return copy
+
+    barrier = pltpu.get_barrier_semaphore()
+    for offset in COLUMN + RING:
+        pl.semaphore_signal(barrier, inc=1, device_id=at(*offset), device_id_type=mesh_id)
+    local = [
+        pltpu.make_async_copy(dos_ref.at[:, column(own * BLOCK, BLOCK)], mine.at[0], local_sem.at[0]),
+        pltpu.make_async_copy(res_ref, residuals.at[0, 0], local_sem.at[1]),
+        pltpu.make_async_copy(list_hbm, list_ref, local_sem.at[2]),
+        pltpu.make_async_copy(slot_hbm, slot_ref, local_sem.at[3]),
+        pltpu.make_async_copy(count_hbm, count_ref, local_sem.at[4]),
+    ]
+    for copy in local:
+        copy.start()
+    pl.semaphore_wait(barrier, len(COLUMN + RING))
+
+    far = []
+    for half in range(HALVES):
+        for dc in range(2):
+            far.append(
+                remote(
+                    dos_ref.at[:, column(flip(c, dc) * BLOCK + half * width, width)],
+                    other.at[half, dc],
+                    far_send.at[half, dc], far_sem.at[half, dc], at(1, 0, 0, dc),
+                )
+            )
+    mate_res = remote(res_ref, residuals.at[1, 0], res_send, res_sem, at(0, 0, 0, 1))
+    mate_block = remote(
+        dos_ref.at[:, column((1 - own) * BLOCK, BLOCK)], mine.at[1], mate_send, mate_sem, at(0, 0, 0, 1)
+    )
+    for copy in local:
+        copy.wait()
+
+    own_slot, far_slot = 2 * y + own, 2 * (1 - y) + c
+    count = jnp.int32(0)
+    for pair in range(4):
+        first = slot_ref[list_ref[0, pair]]
+        second = slot_ref[list_ref[1, pair]]
+        here = ((first == own_slot) & (second == far_slot)) | (
+            (first == far_slot) & (second == own_slot)
+        )
+        count = count + jnp.where(here, count_ref[pair], 0)
+    hot_group = jnp.where(slot_ref[list_ref[0, 0]] >= 2, 1, 0)
+    hot_here = jnp.where(hot_group == y, 1, 0)
+
+    mate_res.wait()
+    both = residuals[0] * residuals[0] + residuals[1] * residuals[1]
+    square_sum[0] = jnp.broadcast_to(jnp.sum(both, axis=1, keepdims=True), (8, 128))
+    started = []
+    for place, offset in enumerate(RING):
+        started.append(
+            remote(
+                square_sum.at[0], square_sum.at[place + 1],
+                sum_send.at[place], sum_sem.at[place], at(*offset),
+            )
+        )
+    for dc in range(2):
+        if dc == 1:
+            mate_block.wait()
+        base = (k - c + flip(c, dc)) * rows
+        live = (base + lax.broadcasted_iota(jnp.int32, (1, rows), 1) < count).astype(jnp.float32)
+        pick = jnp.full((1, rows), hot_here, jnp.int32) == 1
+        weight = residuals[dc]
+        left = mine[dc].T.astype(jnp.float32)
+        left_weighted[dc] = (left * (jnp.where(pick, weight, 1.0) * live)).astype(jnp.bfloat16)
+        left_sq = (left * left).astype(jnp.bfloat16).astype(jnp.float32)
+        left_masked[dc] = (left_sq * live).astype(jnp.bfloat16)
+        right_weight[dc] = jnp.broadcast_to(jnp.where(pick, 1.0, weight), (width, rows)).T
+    for half in range(HALVES):
+        for dc in range(2):
+            far[2 * half + dc].wait()
+            right = other[half, dc].astype(jnp.float32)
+            weighted = (right * right_weight[dc]).astype(jnp.bfloat16)
+            squares = (right * right).astype(jnp.bfloat16)
+            cross_part = jnp.dot(left_weighted[dc], weighted, preferred_element_type=jnp.float32)
+            moment_part = jnp.dot(left_masked[dc], squares, preferred_element_type=jnp.float32)
+            if dc == 0:
+                cross[half] = cross_part.reshape(8, share, width)
+                moment[half] = moment_part.reshape(8, share, width)
+            else:
+                cross_all = cross[half] + cross_part.reshape(8, share, width)
+                moment_all = moment[half] + moment_part.reshape(8, share, width)
+                cross[half] = cross_all
+                moment[half] = moment_all
+                parts[half, :, :share, :] = cross_all.astype(jnp.bfloat16)
+                parts[half, :, share:, :] = moment_all.astype(jnp.bfloat16)
+        for place, offset in enumerate(RING):
+            to = at(*offset)
+            started.append(
+                remote(
+                    parts.at[half, to[1] // 2], parts_in.at[half, place],
+                    part_send.at[half, place], part_sem.at[half, place], to,
+                )
+            )
+    for copy in started[: len(RING)]:
+        copy.wait()
+    total = square_sum[0]
+    for place in range(len(RING)):
+        total += square_sum[place + 1]
+    spread_var = total[0:1, 0:1] / (rows * 16)
+    row_sums = jnp.zeros((share, 1), jnp.float32)
+    for half in range(HALVES):
+        cross_sum = cross[half, k // 2]
+        moment_sum = moment[half, k // 2]
+        for place in range(len(RING)):
+            started[(1 + half) * len(RING) + place].wait()
+            cross_sum += parts_in[half, place, :share, :].astype(jnp.float32)
+            moment_sum += parts_in[half, place, share:, :].astype(jnp.float32)
+        zvalue = cross_sum / jnp.sqrt(spread_var * moment_sum + 1e-06)
+        row_sums += jnp.sum(zvalue, axis=1, keepdims=True)
+        vecs[1, :, half * width : (half + 1) * width] = jnp.sum(zvalue, axis=0, keepdims=True)
+    row_at = lax.broadcasted_iota(jnp.int32, (share, BLOCK), 0) + share * (k // 2)
+    spot = row_at == lax.broadcasted_iota(jnp.int32, (share, BLOCK), 1)
+    vecs[0] = jnp.sum(jnp.where(spot, row_sums, 0.0), axis=0, keepdims=True)
+    started = []
+    for place, offset in enumerate(RING):
+        started.append(
+            remote(vecs, vecs_in.at[place], vec_send.at[place], vec_sem.at[place], at(*offset))
+        )
+    total = vecs[...]
+    for place in range(len(RING)):
+        started[place].wait()
+        total += vecs_in[place]
+    last[...] = total
+    started = []
+    for place, offset in enumerate(COLUMN):
+        started.append(
+            remote(
+                last.at[offset[0]], last_in.at[place],
+                last_send.at[place], last_sem.at[place], at(*offset),
+            )
+        )
+    for copy in started:
+        copy.wait()
+    swap_far = jnp.full((1, BLOCK), c, jnp.int32) == 1
+    swap_own = jnp.full((1, BLOCK), own, jnp.int32) == 1
+    by_own = [last[0], last_in[0]]
+    by_far = [last_in[1], last_in[2]]
+    scale = 1.0 / math.sqrt(2 * BLOCK)
+    for block in range(2):
+        same = jnp.where(swap_own, by_own[1 - block], by_own[block])
+        cross_group = jnp.where(swap_far, by_far[1 - block], by_far[block])
+        out_ref[block : block + 1, :] = (same + cross_group) * scale
+
+
+def two_groups(dosages, residual, pair_list, block_slot, pair_counts):
+    rows = dosages.shape[0]
+    width = BLOCK // HALVES
+    dma = pltpu.SemaphoreType.DMA
+    peers = len(RING)
+    hbm = pl.BlockSpec(memory_space=pltpu.HBM)
+    half_type, full_type = jnp.bfloat16, jnp.float32
+    score = pl.pallas_call(
+        two_groups_kernel,
+        out_shape=jax.ShapeDtypeStruct((2, BLOCK), jnp.float32),
+        in_specs=[hbm, hbm, hbm, hbm, hbm],
+        out_specs=pl.BlockSpec(memory_space=pltpu.VMEM),
+        scratch_shapes=[
+            pltpu.SMEM((2, 4), jnp.int32),
+            pltpu.SMEM((4,), jnp.int32),
+            pltpu.SMEM((4,), jnp.int32),
+            pltpu.VMEM((2, rows, BLOCK), half_type),
+            pltpu.VMEM((HALVES, 2, rows, width), half_type),
+            pltpu.VMEM((2, 1, rows), full_type),
+            pltpu.VMEM((2, BLOCK, rows), half_type),
+            pltpu.VMEM((2, BLOCK, rows), half_type),
+            pltpu.VMEM((2, rows, width), full_type),
+            pltpu.VMEM((peers + 1, 8, 128), full_type),
+            pltpu.VMEM((HALVES, 8, BLOCK // 8, width), full_type),
+            pltpu.VMEM((HALVES, 8, BLOCK // 8, width), full_type),
+            pltpu.VMEM((HALVES, 8, BLOCK // 4, width), half_type),
+            pltpu.VMEM((HALVES, peers, BLOCK // 4, width), half_type),
+            pltpu.VMEM((2, 1, BLOCK), full_type),
+            pltpu.VMEM((peers, 2, 1, BLOCK), full_type),
+            pltpu.VMEM((2, 1, BLOCK), full_type),
+            pltpu.VMEM((3, 1, BLOCK), full_type),
+            dma((5,)), dma, dma, dma((HALVES, 2)), dma((HALVES, 2)), dma, dma,
+            dma((peers,)), dma((peers,)), dma((HALVES, peers)), dma((HALVES, peers)),
+            dma((peers,)), dma((peers,)), dma((3,)), dma((3,)),
+        ],
+        compiler_params=pltpu.CompilerParams(
+            collective_id=0, has_side_effects=True, vmem_limit_bytes=32 * 1024 * 1024
+        ),
+        name="pair_scores",
+    )(pair_list.T, block_slot, pair_counts, dosages, residual)
+    return score.reshape(2 * BLOCK)
+
+
 def solution(mesh):
+    def on_device(dosages, residual, pair_list, block_slot, pair_counts):
+        groups, shards = lax.axis_size("snp"), lax.axis_size("samp")
+        fits = groups == 2 and shards == 16 and block_slot.shape[0] == 4
+        run = two_groups if fits else any_groups
+        return run(dosages, residual, pair_list, block_slot, pair_counts)
+
     return jax.shard_map(
         on_device,
         mesh=mesh,

time: 157 us -> 40.9 us (0.26)
  blocking collectives: 68.3 us -> 0 us
  waiting for transfers between devices: 50.1 us -> 0 us
  Pallas kernels: 0 us -> 36.9 us
  between operations: 14.8 us -> 0.01 us
  other arithmetic: 7 us -> 0 us
  matrix products: 6.34 us -> 0 us
  loops' own time: 3.83 us -> 0 us
  local copies, waits for them, and re-layouts: 6.29 us -> 3.75 us
    psum x2 -> x0, blocking collectives: 63.3 us -> none  [the longest x1 33.9 us: on_device(): spread_sum = lax.psum(jnp.sum(residual * residual), 'samp')]
    pallas_call x0 -> x1, Pallas kernels: none -> 36.9 us  [two_groups(): pl.pallas_call(two_groups_kernel, out_shape=jax.ShapeDtypeStruct((2, BLOC...]
    all_gather x1 -> x0, waiting for transfers between devices: 28.2 us -> none  [on_device(): gathered = lax.all_gather(dosages, 'snp', axis=1, tiled=True)]
    reduce_scatter x1 -> x0, waiting for transfers between devices: 21.1 us -> none  [on_device(): lax.psum_scatter(lax.fori_loop(0, width_slots, one_slot, start_buffer), '...]
    dot_general x6 -> x0, matrix products: 6.34 us -> none  [the longest x2 3.19 us: one_slot(): jnp.einsum('si,sj->ij', weighted, right, preferred_element_type=jnp.float32)]
    unnamed x1 -> x0, blocking collectives: 4.95 us -> none
    another operation x2 -> x0, loops' own time: 3.83 us -> none  [the longest x1 2.55 us: on_device(): lax.fori_loop(0, width_slots, one_slot, start_buffer)]
    dynamic_slice x10 -> x0, local copies, waits for them, and re-layouts: 3.77 us -> none  [the longest x4 1.27 us: on_device(): masked = lax.map(masked_block, (second_at, live_rows))]
  transfers between devices with their start and end apart: 2 -> 0, of which waited for: 2 -> 0; matrix products, arithmetic and copies ran while one was open for 3% -> 0% of each run, Pallas kernels for 0% -> 0%
where the time goes in v2:
time: 40.9 us; the launch traced here: 40.7 us
  Pallas kernels  36.9 us (90%)
  local copies, waits for them, and re-layouts  3.75 us (9%)
    pallas_call x1, Pallas kernels, two_groups(): pl.pallas_call(two_groups_kernel, out_shape=jax.ShapeDtypeStruct((2, BLOC...  36.9 us
    unnamed x11, local copies, waits for them, and re-layouts  3.75 us

profile of v2, /device:TPU:0, one launch (start us, length us, event | category | flops | bytes accessed | tf_op | source)
XLA Modules:
  0.0 40.7 jit_solution(1422858306495203967)
XLA Ops:
  0.0 0.0 copy-start.3
  0.0 0.0 copy-start.2
  0.0 0.7 %copy-done.3 = s32[4]{0:T(128)S(1)} copy-done((s32[4]{0:T(128)S(1)}, s32[4]{0:T(128)}, u32[]{:S(2)}) %copy-start.3) | copy-done | bytes 40
  0.7 0.0 copy-done.2
  0.7 0.0 copy-start
  0.7 1.1 %copy-done = bf16[768,512]{1,0:T(8,128)(2,1)S(1)} copy-done((bf16[768,512]{1,0:T(8,128)(2,1)S(1)}, bf16[768,512]{1,0:T(8,128)(2,1)}, u32[]{:S(2)}) %copy-start) | copy-done | bytes 786456
  1.8 0.0 copy-start.1
  1.8 0.7 %copy-done.1 = f32[768]{0:T(1024)S(1)} copy-done((f32[768]{0:T(1024)S(1)}, f32[768]{0:T(1024)}, u32[]{:S(2)}) %copy-start.1) | copy-done | bytes 3096
  2.5 0.0 copy-start.4
  2.5 0.7 %copy-done.4 = s32[4]{0:T(128)S(1)} copy-done((s32[4]{0:T(128)S(1)}, s32[4]{0:T(128)}, u32[]{:S(2)}) %copy-start.4) | copy-done | bytes 40
  3.2 36.9 %pair_scores.1 = f32[2,256]{1,0:T(2,128)S(1)} custom-call(s32[2,4]{1,0:T(2,128)S(1)} %bitcast.4, s32[4]{0:T(128)S(1)} %copy-done.3, s32[4]{0:T(128)S(1)} %copy-done.4, bf16[768,512]{1,0:T(8,128)(2,1)S(1)} %copy-done, f32[768]{0:T(1024)S(1)} %copy-done.1), custom_call_target="tpu_custom_call" | custom-call | tf_op jit(solution)/shard_map/pair_scores/pallas_call | solution.py:285
  40.1 0.6 %copy.6 = f32[1,2,2,128]{3,1,2,0:T(2,128)} copy(f32[1,2,2,128]{3,2,1,0:T(2,128)S(1)} %bitcast.3) | data formatting | bytes 4096
Async XLA Ops:
  0.0 0.7 %copy-start.3 = (s32[4]{0:T(128)S(1)}, s32[4]{0:T(128)}, u32[]{:S(2)}) copy-start(s32[4]{0:T(128)} %slot_hbm.1) | copy-start | bytes 52
  0.0 0.7 %copy-start.2 = (s32[4,2]{0,1:T(2,128)S(1)}, s32[4,2]{0,1:T(2,128)}, u32[]{:S(2)}) copy-start(s32[4,2]{0,1:T(2,128)} %param.7) | copy-start | bytes 100
  0.7 1.1 %copy-start = (bf16[768,512]{1,0:T(8,128)(2,1)S(1)}, bf16[768,512]{1,0:T(8,128)(2,1)}, u32[]{:S(2)}) copy-start(bf16[768,512]{1,0:T(8,128)(2,1)} %dos_ref.1) | copy-start | bytes 2359300
  1.8 0.7 %copy-start.1 = (f32[768]{0:T(1024)S(1)}, f32[768]{0:T(1024)}, u32[]{:S(2)}) copy-start(f32[768]{0:T(1024)} %res_ref.1) | copy-start | bytes 9220
  2.5 0.7 %copy-start.4 = (s32[4]{0:T(128)S(1)}, s32[4]{0:T(128)}, u32[]{:S(2)}) copy-start(s32[4]{0:T(128)} %count_hbm.1) | copy-start | bytes 52

commit v3 on v2

--- a/solution.py
+++ b/solution.py
@@ -96,6 +96,7 @@
 HALVES = 2
 RING = [(0, dz, dx, 0) for dz in range(4) for dx in range(2)][1:]
 COLUMN = [(0, 0, 0, 1), (1, 0, 0, 0), (1, 0, 0, 1)]
+CHIPS = [(dy, dz, dx, 0) for dy in range(2) for dz in range(4) for dx in range(2)][1:]
 
 
 def flip(bit, change):
@@ -105,9 +106,9 @@
 def two_groups_kernel(
     list_hbm, slot_hbm, count_hbm, dos_ref, res_ref, out_ref,
     list_ref, slot_ref, count_ref, mine, other, residuals, left_weighted, left_masked, right_weight,
-    square_sum, cross, moment, parts, parts_in, vecs, vecs_in, last, last_in,
+    square_sum, cross, moment, parts, parts_in, vecs, vecs_in, chip, chip_in,
     local_sem, mate_sem, mate_send, far_sem, far_send, res_sem, res_send,
-    sum_sem, sum_send, part_sem, part_send, vec_sem, vec_send, last_sem, last_send,
+    sum_sem, sum_send, part_sem, part_send, vec_sem, vec_send, chip_sem, chip_send, round_sem,
 ):
     y = lax.axis_index("snp")
     k = lax.axis_index("samp")
@@ -132,9 +133,28 @@
         copy.start()
         return copy
 
+    def take(sem, like):
+        pltpu.make_async_copy(like, like, sem).wait()
+
+    def greet(sem, *offset):
+        pl.semaphore_signal(sem, inc=1, device_id=at(*offset), device_id_type=mesh_id)
+
+    def greet_neighbours(sem):
+        greet(sem, 0, 0, 1, 0)
+
+        @pl.when(z > 0)
+        def _():
+            greet(sem, 0, 3, 0, 0)
+
+        @pl.when(z < 3)
+        def _():
+            greet(sem, 0, 1, 0, 0)
+
+    neighbours = 1 + jnp.where(z > 0, 1, 0) + jnp.where(z < 3, 1, 0)
     barrier = pltpu.get_barrier_semaphore()
-    for offset in COLUMN + RING:
-        pl.semaphore_signal(barrier, inc=1, device_id=at(*offset), device_id_type=mesh_id)
+    for offset in COLUMN:
+        greet(barrier, *offset)
+    greet_neighbours(barrier)
     local = [
         pltpu.make_async_copy(dos_ref.at[:, column(own * BLOCK, BLOCK)], mine.at[0], local_sem.at[0]),
         pltpu.make_async_copy(res_ref, residuals.at[0, 0], local_sem.at[1]),
@@ -144,7 +164,7 @@
     ]
     for copy in local:
         copy.start()
-    pl.semaphore_wait(barrier, len(COLUMN + RING))
+    pl.semaphore_wait(barrier, len(COLUMN) + neighbours)
 
     far = []
     for half in range(HALVES):
@@ -160,6 +180,7 @@
     mate_block = remote(
         dos_ref.at[:, column((1 - own) * BLOCK, BLOCK)], mine.at[1], mate_send, mate_sem, at(0, 0, 0, 1)
     )
+    greet_neighbours(round_sem.at[0])
     for copy in local:
         copy.wait()
 
@@ -175,20 +196,12 @@
     hot_group = jnp.where(slot_ref[list_ref[0, 0]] >= 2, 1, 0)
     hot_here = jnp.where(hot_group == y, 1, 0)
 
-    mate_res.wait()
-    both = residuals[0] * residuals[0] + residuals[1] * residuals[1]
-    square_sum[0] = jnp.broadcast_to(jnp.sum(both, axis=1, keepdims=True), (8, 128))
-    started = []
-    for place, offset in enumerate(RING):
-        started.append(
-            remote(
-                square_sum.at[0], square_sum.at[place + 1],
-                sum_send.at[place], sum_sem.at[place], at(*offset),
-            )
-        )
     for dc in range(2):
         if dc == 1:
-            mate_block.wait()
+            pl.semaphore_wait(round_sem.at[0], neighbours)
+            greet_neighbours(round_sem.at[1])
+            mate_res.wait_recv()
+            mate_block.wait_recv()
         base = (k - c + flip(c, dc)) * rows
         live = (base + lax.broadcasted_iota(jnp.int32, (1, rows), 1) < count).astype(jnp.float32)
         pick = jnp.full((1, rows), hot_here, jnp.int32) == 1
@@ -198,9 +211,18 @@
         left_sq = (left * left).astype(jnp.bfloat16).astype(jnp.float32)
         left_masked[dc] = (left_sq * live).astype(jnp.bfloat16)
         right_weight[dc] = jnp.broadcast_to(jnp.where(pick, 1.0, weight), (width, rows)).T
+    pl.semaphore_wait(round_sem.at[1], neighbours)
+    greet_neighbours(round_sem.at[2])
+    pl.semaphore_wait(round_sem.at[2], neighbours)
+    greet(round_sem.at[3], 1, 0, 0, 0)
+    both = residuals[0] * residuals[0] + residuals[1] * residuals[1]
+    square_sum[0] = jnp.broadcast_to(jnp.sum(both, axis=1, keepdims=True), (8, 128))
+    for place, offset in enumerate(RING):
+        remote(square_sum.at[0], square_sum.at[place + 1], sum_send, sum_sem, at(*offset))
+    pl.semaphore_wait(round_sem.at[3], 1)
     for half in range(HALVES):
         for dc in range(2):
-            far[2 * half + dc].wait()
+            far[2 * half + dc].wait_recv()
             right = other[half, dc].astype(jnp.float32)
             weighted = (right * right_weight[dc]).astype(jnp.bfloat16)
             squares = (right * right).astype(jnp.bfloat16)
@@ -218,14 +240,12 @@
                 parts[half, :, share:, :] = moment_all.astype(jnp.bfloat16)
         for place, offset in enumerate(RING):
             to = at(*offset)
-            started.append(
-                remote(
-                    parts.at[half, to[1] // 2], parts_in.at[half, place],
-                    part_send.at[half, place], part_sem.at[half, place], to,
-                )
+            remote(
+                parts.at[half, to[1] // 2], parts_in.at[half, place],
+                part_send.at[half], part_sem.at[half], to,
             )
-    for copy in started[: len(RING)]:
-        copy.wait()
+    others = square_sum.at[pl.ds(1, len(RING))]
+    take(sum_sem, others)
     total = square_sum[0]
     for place in range(len(RING)):
         total += square_sum[place + 1]
@@ -234,8 +254,8 @@
     for half in range(HALVES):
         cross_sum = cross[half, k // 2]
         moment_sum = moment[half, k // 2]
+        take(part_sem.at[half], parts_in.at[half])
         for place in range(len(RING)):
-            started[(1 + half) * len(RING) + place].wait()
             cross_sum += parts_in[half, place, :share, :].astype(jnp.float32)
             moment_sum += parts_in[half, place, share:, :].astype(jnp.float32)
         zvalue = cross_sum / jnp.sqrt(spread_var * moment_sum + 1e-06)
@@ -244,35 +264,25 @@
     row_at = lax.broadcasted_iota(jnp.int32, (share, BLOCK), 0) + share * (k // 2)
     spot = row_at == lax.broadcasted_iota(jnp.int32, (share, BLOCK), 1)
     vecs[0] = jnp.sum(jnp.where(spot, row_sums, 0.0), axis=0, keepdims=True)
-    started = []
-    for place, offset in enumerate(RING):
-        started.append(
-            remote(vecs, vecs_in.at[place], vec_send.at[place], vec_sem.at[place], at(*offset))
-        )
-    total = vecs[...]
-    for place in range(len(RING)):
-        started[place].wait()
-        total += vecs_in[place]
-    last[...] = total
-    started = []
-    for place, offset in enumerate(COLUMN):
-        started.append(
-            remote(
-                last.at[offset[0]], last_in.at[place],
-                last_send.at[place], last_sem.at[place], at(*offset),
-            )
-        )
-    for copy in started:
-        copy.wait()
-    swap_far = jnp.full((1, BLOCK), c, jnp.int32) == 1
-    swap_own = jnp.full((1, BLOCK), own, jnp.int32) == 1
-    by_own = [last[0], last_in[0]]
-    by_far = [last_in[1], last_in[2]]
-    scale = 1.0 / math.sqrt(2 * BLOCK)
-    for block in range(2):
-        same = jnp.where(swap_own, by_own[1 - block], by_own[block])
-        cross_group = jnp.where(swap_far, by_far[1 - block], by_far[block])
-        out_ref[block : block + 1, :] = (same + cross_group) * scale
+    mate_vecs = remote(vecs, vecs_in, vec_send, vec_sem, at(0, 0, 0, 1))
+    mate_vecs.wait_recv()
+    for group, block_here in ((0, own), (1, c)):
+        here, there = vecs[group], vecs_in[group]
+        for block in range(2):
+            pick = jnp.full((1, BLOCK), block_here, jnp.int32) == block
+            chip[group, block : block + 1, :] = jnp.where(pick, here, there)
+    for place, offset in enumerate(CHIPS):
+        remote(chip.at[offset[0]], chip_in.at[place + 1], chip_send, chip_sem, at(*offset))
+    chip_in[0] = chip[0]
+    other_chips = chip_in.at[pl.ds(1, len(CHIPS))]
+    take(chip_sem, other_chips)
+    out_ref[...] = jnp.sum(chip_in[...], axis=0) * (1.0 / math.sqrt(2 * BLOCK))
+    for copy in far + [mate_res, mate_block, mate_vecs]:
+        copy.wait_send()
+    take(sum_send, others)
+    for half in range(HALVES):
+        take(part_send.at[half], parts_in.at[half])
+    take(chip_send, other_chips)
 
 
 def two_groups(dosages, residual, pair_list, block_slot, pair_counts):
@@ -303,15 +313,15 @@
             pltpu.VMEM((HALVES, 8, BLOCK // 4, width), half_type),
             pltpu.VMEM((HALVES, peers, BLOCK // 4, width), half_type),
             pltpu.VMEM((2, 1, BLOCK), full_type),
-            pltpu.VMEM((peers, 2, 1, BLOCK), full_type),
             pltpu.VMEM((2, 1, BLOCK), full_type),
-            pltpu.VMEM((3, 1, BLOCK), full_type),
+            pltpu.VMEM((2, 2, BLOCK), full_type),
+            pltpu.VMEM((len(CHIPS) + 1, 2, BLOCK), full_type),
             dma((5,)), dma, dma, dma((HALVES, 2)), dma((HALVES, 2)), dma, dma,
-            dma((peers,)), dma((peers,)), dma((HALVES, peers)), dma((HALVES, peers)),
-            dma((peers,)), dma((peers,)), dma((3,)), dma((3,)),
+            dma, dma, dma((HALVES,)), dma((HALVES,)), dma, dma, dma, dma,
+            pltpu.SemaphoreType.REGULAR((4,)),
         ],
         compiler_params=pltpu.CompilerParams(
-            collective_id=0, has_side_effects=True, vmem_limit_bytes=32 * 1024 * 1024
+            collective_id=0, has_side_effects=True, vmem_limit_bytes=62 * 1024 * 1024
         ),
         name="pair_scores",
     )(pair_list.T, block_slot, pair_counts, dosages, residual)

time: 40.9 us -> 35.5 us (0.87)
  Pallas kernels: 36.9 us -> 34.1 us
  local copies, waits for them, and re-layouts: 3.75 us -> 1.26 us
    pallas_call x1, Pallas kernels: 36.9 us -> 34.1 us  [two_groups(): pl.pallas_call(two_groups_kernel, out_shape=jax.ShapeDtypeStruct((2, BLOC...]
    unnamed x11 -> x1, local copies, waits for them, and re-layouts: 3.75 us -> 1.26 us
where the time goes in v3:
time: 35.5 us; the launch traced here: 35.4 us
  Pallas kernels  34.1 us (96%)
  local copies, waits for them, and re-layouts  1.26 us (4%)
    pallas_call x1, Pallas kernels, two_groups(): pl.pallas_call(two_groups_kernel, out_shape=jax.ShapeDtypeStruct((2, BLOC...  34.1 us
    unnamed x1, local copies, waits for them, and re-layouts  1.26 us

profile of v3, /device:TPU:0, one launch (start us, length us, event | category | flops | bytes accessed | tf_op | source)
XLA Modules:
  0.0 35.4 jit_solution(17756613216654847696)
XLA Ops:
  0.0 34.1 %pair_scores.1 = f32[2,256]{1,0:T(2,128)} custom-call(s32[2,4]{1,0:T(2,128)} %bitcast.4, s32[4]{0:T(128)} %slot_hbm.1, s32[4]{0:T(128)} %count_hbm.1, bf16[768,512]{1,0:T(8,128)(2,1)} %dos_ref.1, f32[768]{0:T(1024)} %res_ref.1), custom_call_target="tpu_custom_call" | custom-call | tf_op jit(solution)/shard_map/pair_scores/pallas_call | solution.py:295
  34.1 1.3 %copy.6 = f32[1,2,2,128]{3,1,2,0:T(2,128)} copy(f32[1,2,2,128]{3,2,1,0:T(2,128)} %bitcast.3) | data formatting | bytes 4096

commit v4 on v3

--- a/solution.py
+++ b/solution.py
@@ -276,7 +276,10 @@
     chip_in[0] = chip[0]
     other_chips = chip_in.at[pl.ds(1, len(CHIPS))]
     take(chip_sem, other_chips)
-    out_ref[...] = jnp.sum(chip_in[...], axis=0) * (1.0 / math.sqrt(2 * BLOCK))
+    score = jnp.sum(chip_in[...], axis=0) * (1.0 / math.sqrt(2 * BLOCK))
+    for row in range(4):
+        lane = row % 2 * 128
+        out_ref[row : row + 1, :] = score[row // 2 : row // 2 + 1, lane : lane + 128]
     for copy in far + [mate_res, mate_block, mate_vecs]:
         copy.wait_send()
     take(sum_send, others)
@@ -294,7 +297,7 @@
     half_type, full_type = jnp.bfloat16, jnp.float32
     score = pl.pallas_call(
         two_groups_kernel,
-        out_shape=jax.ShapeDtypeStruct((2, BLOCK), jnp.float32),
+        out_shape=jax.ShapeDtypeStruct((BLOCK // 64, 128), jnp.float32),
         in_specs=[hbm, hbm, hbm, hbm, hbm],
         out_specs=pl.BlockSpec(memory_space=pltpu.VMEM),
         scratch_shapes=[

time: 35.5 us -> 35.5 us (level)
  no operation moved by 1% of the time
where the time goes in v4:
time: 35.5 us; the launch traced here: 35.4 us
  Pallas kernels  34.1 us (96%)
  local copies, waits for them, and re-layouts  1.26 us (4%)
    pallas_call x1, Pallas kernels, two_groups(): pl.pallas_call(two_groups_kernel, out_shape=jax.ShapeDtypeStruct((BLOCK /...  34.1 us
    unnamed x1, local copies, waits for them, and re-layouts  1.26 us

profile of v4, /device:TPU:0, one launch (start us, length us, event | category | flops | bytes accessed | tf_op | source)
XLA Modules:
  0.0 35.4 jit_solution(1559801500893113385)
XLA Ops:
  0.0 34.1 %pair_scores.1 = f32[4,128]{1,0:T(4,128)} custom-call(s32[2,4]{1,0:T(2,128)} %bitcast.3, s32[4]{0:T(128)} %slot_hbm.1, s32[4]{0:T(128)} %count_hbm.1, bf16[768,512]{1,0:T(8,128)(2,1)} %dos_ref.1, f32[768]{0:T(1024)} %res_ref.1), custom_call_target="tpu_custom_call" | custom-call | tf_op jit(solution)/shard_map/pair_scores/pallas_call | solution.py:298
  34.1 1.3 %copy.7 = f32[512]{0:T(512)} copy(f32[512]{0:T(512)} %bitcast.2) | data formatting | bytes 4096
